TPU v7x, 32 devices: a whole 2x2x4 slice. The times are simulated.
32 devices in a mesh: parts: 2 (over y), wide: 4 (over z), blk: 2 (over x), sub: 2 (over core).
Axes of the slice: x: 2, y: 2, z: 4, core: 2. Of those that a mesh axis runs over, the one named last changes fastest.
Arguments:
- embeddings: bfloat16 [6144, 768], P(('parts', 'wide', 'blk', 'sub')), parts along dimension 0, may hold values from -16 to 16
- cluster_ids: int32 [6144], P(('parts', 'wide', 'blk', 'sub')), parts along dimension 0, may hold values from 0 to 63, as said below
- cluster_slot: int32 [128], P('parts'), parts along dimension 0, may hold values from 0 to 63, each once
Outputs:
- row_max: float32 [6144], P(('parts', 'wide', 'blk', 'sub')), parts along dimension 0
- cluster_best: float32 [128], P(('parts', 'wide')), parts along dimension 0
There are 2 independent parts, one for each index of `parts`. A program takes and returns all parts, laid end to end along the dimension named above; each array names one. Nothing has to cross between parts.
Inputs may be any that keep to these rules, and one draw needn't show every extreme that they name: `cluster_ids`: in each aligned block of 192 rows (the rows of one device) no cluster is named more than 4 times, and some cluster exactly 4 times. `cluster_slot`: each slot is given to exactly one cluster.
All inputs are finite; a program needn't handle non-finite values.
Results may differ from a plain program's by a relative error of at most 0.00071.
Values may be sent and summed in bfloat16 or wider, within the bound.
A program may use at most 64 MiB of HBM per device.

v0:
```python
import jax
import jax.numpy as jnp
from jax import lax
from jax.sharding import PartitionSpec as P

CAP = 4


EPSILON = 1e-06
LOW_MARK = -2.0


def unit_rows(embeddings):
    values = embeddings.astype(jnp.float32)
    squares = jnp.sum(values * values, axis=1, keepdims=True)
    return (values * lax.rsqrt(squares + EPSILON)).astype(jnp.bfloat16)


def best_match(queries, best_sofar, pieces):
    key_rows, key_marks = pieces
    scores = jnp.einsum("csd,ctd->cst", queries, key_rows, preferred_element_type=jnp.float32)
    query_index = jnp.arange(queries.shape[1], dtype=jnp.int32)
    key_index = jnp.arange(key_rows.shape[1], dtype=jnp.int32)
    usable = (key_marks[:, None, :] > 0) & (query_index[:, None] != key_index[None, :])[None, :, :]
    return jnp.maximum(best_sofar, jnp.max(jnp.where(usable, scores, LOW_MARK), axis=2))


def local(embeddings, cluster_ids, cluster_slot):
    row_count = embeddings.shape[0]
    feature_count = embeddings.shape[1]
    wide_size = lax.axis_size("wide")
    cluster_count = cluster_slot.shape[0]
    owned_count = cluster_count // wide_size
    span_slots = wide_size * CAP
    total_slots = owned_count * span_slots
    normed = unit_rows(embeddings)
    row_iota = jnp.arange(row_count, dtype=jnp.int32)
    same_cluster = cluster_ids[:, None] == cluster_ids[None, :]
    earlier = row_iota[None, :] < row_iota[:, None]
    rank_in = jnp.sum(same_cluster & earlier, axis=1, dtype=jnp.int32)
    matches = cluster_ids[:, None] == jnp.arange(cluster_count, dtype=jnp.int32)[None, :]
    placed = jnp.sum(jnp.where(matches, cluster_slot[None, :], 0), axis=1, dtype=jnp.int32)
    target = (placed % owned_count * wide_size + placed // owned_count) * CAP + rank_in
    outgoing = jnp.zeros((total_slots, feature_count), jnp.bfloat16).at[target].set(normed)
    occupied = jnp.zeros((total_slots,), jnp.bfloat16).at[target].set(1.0)
    outgoing = outgoing.reshape(owned_count, wide_size, CAP, feature_count)
    occupied = occupied.reshape(owned_count, wide_size, CAP)
    arrived, present = (
        lax.all_to_all(outgoing, "wide", split_axis=1, concat_axis=1, tiled=True),
        lax.all_to_all(occupied, "wide", split_axis=1, concat_axis=1, tiled=True),
    )
    arrived = arrived.reshape(owned_count, span_slots, feature_count)
    present = present.reshape(owned_count, span_slots)
    single_rows, single_marks = (
        lax.all_to_all(arrived, ("blk", "sub"), split_axis=0, concat_axis=1, tiled=True),
        lax.all_to_all(present, ("blk", "sub"), split_axis=0, concat_axis=1, tiled=True),
    )
    single_start = jnp.full(single_marks.shape, -1.0, jnp.float32)
    single_best = best_match(single_rows, single_start, (single_rows, single_marks))
    best_slot = lax.all_to_all(single_best, ("blk", "sub"), split_axis=1, concat_axis=0, tiled=True)
    peak_local = jnp.max(jnp.where(present > 0, best_slot, -1.0), axis=1)
    cluster_best = lax.pmax(peak_local, ("blk", "sub"))
    returned = lax.all_to_all(
        best_slot.reshape(owned_count, wide_size, CAP),
        "wide",
        split_axis=1,
        concat_axis=1,
        tiled=True,
    )
    row_max = returned.reshape(total_slots)[target]
    return (row_max, cluster_best)


def solution(mesh):
    return jax.shard_map(
        local,
        mesh=mesh,
        in_specs=(
            P(("parts", "wide", "blk", "sub"), None),
            P(("parts", "wide", "blk", "sub")),
            P("parts"),
        ),
        out_specs=(P(("parts", "wide", "blk", "sub")), P(("parts", "wide"))),
        check_vma=False,
    )
```

profile of v0, /device:TPU:0, one launch (start us, length us, event | category | flops | bytes accessed | tf_op | source)
XLA Modules:
  0.0 70.0 jit_solution(6384720680271592082)
XLA Ops:
  0.7 1.0 %convert_reduce_fusion = s32[192]{0:T(256)S(1)} fusion(s32[192]{0:T(256)} %param.4), kind=kLoop, calls=%fused_computation.12 | loop fusion | flops 184128 | bytes 1536 | tf_op jit(solution)/shard_map/reduce_sum | solution.py:40
  1.8 1.8 %scatter_custom_fusion = bf16[256]{0:T(256)(128)(2,1)S(1)} fusion(s32[192]{0:T(256)S(1)} %bitcast.18, bf16[192]{0:T(256)(128)(2,1)S(1)} %broadcast.141, bf16[]{:T(256)} %constant.16.clone.1), kind=kCustom, calls=%fused_computation.31 | custom fusion | bytes 514 | tf_op jit(solution)/shard_map/scatter | solution.py:45
  3.7 0.7 %copy.18 = bf16[16,4,4]{0,2,1:T(4,128)(2,1)} copy(bf16[16,4,4]{2,1,0:T(4,128)(2,1)S(1)} %reshape.157) | data formatting | bytes 1024 | tf_op jit(solution)/shard_map/reshape | solution.py:47
  4.4 6.3 %all-to-all-start = ((bf16[16,4,4]{0,2,1:T(4,128)(2,1)}), bf16[16,4,4]{0,2,1:T(4,128)(2,1)S(1)}, u32[]{:S(2)}, u32[]{:S(2)}) async-start(bf16[16,4,4]{0,2,1:T(4,128)(2,1)} %copy.18), calls=%async_computation | async-start | bytes 8192 | tf_op jit(solution)/shard_map/all_to_all | solution.py:50
  10.7 1.1 %fusion.1 = f32[192]{0:T(256)S(1)} fusion(bf16[192,768]{1,0:T(8,128)(2,1)} %param.3), kind=kLoop, calls=%fused_computation.7 | loop fusion | flops 442176 | bytes 295680 | tf_op jit(solution)/shard_map/reduce_sum | solution.py:15
  11.8 1.6 %scatter_custom_fusion.1 = bf16[256,768]{1,0:T(8,128)(2,1)S(1)} fusion(s32[192]{0:T(256)S(1)} %bitcast.19, bf16[192,768]{1,0:T(8,128)(2,1)S(1)} %copy-done, f32[192]{0:T(256)S(1)} %add_rsqrt_fusion, bf16[]{:T(256)} %constant.16.clone.1), kind=kCustom, calls=%fused_computation.9 | custom fusion | flops 442368 | bytes 689154 | tf_op jit(solution)/shard_map/scatter | solution.py:44
  13.5 0.9 %copy.21 = bf16[16,4,4,768]{3,2,0,1:T(4,128)(2,1)} copy(bf16[16,4,4,768]{3,2,1,0:T(4,128)(2,1)S(1)} %reshape.158) | data formatting | bytes 786432 | tf_op jit(solution)/shard_map/reshape | solution.py:46
  14.4 1.9 %all-to-all-done = bf16[16,4,4]{0,2,1:T(4,128)(2,1)S(1)} async-done(((bf16[16,4,4]{0,2,1:T(4,128)(2,1)}), bf16[16,4,4]{0,2,1:T(4,128)(2,1)S(1)}, u32[]{:S(2)}, u32[]{:S(2)}) %all-to-all-start) | async-done | bytes 544 | tf_op jit(solution)/shard_map/all_to_all | solution.py:50
  16.3 3.5 %all-to-all-start.2 = ((bf16[16,4,4,768]{3,2,0,1:T(4,128)(2,1)}), bf16[16,4,4,768]{3,2,0,1:T(4,128)(2,1)S(1)}, u32[]{:S(2)}, u32[]{:S(2)}) async-start(bf16[16,4,4,768]{3,2,0,1:T(4,128)(2,1)} %copy.21), calls=%async_computation.2 | async-start | bytes 786432 | tf_op jit(solution)/shard_map/all_to_all | solution.py:49
  19.8 0.7 copy.27
  20.5 10.1 %all-to-all-done.2 = bf16[16,4,4,768]{3,2,0,1:T(4,128)(2,1)S(1)} async-done(((bf16[16,4,4,768]{3,2,0,1:T(4,128)(2,1)}), bf16[16,4,4,768]{3,2,0,1:T(4,128)(2,1)S(1)}, u32[]{:S(2)}, u32[]{:S(2)}) %all-to-all-start.2) | async-done | bytes 393248 | tf_op jit(solution)/shard_map/all_to_all | solution.py:49
  30.6 3.2 %all-to-all-start.1 = ((bf16[4,4,16]{2,1,0:T(4,128)(2,1)}), bf16[4,4,16]{2,1,0:T(4,128)(2,1)S(1)}, u32[]{:S(2)}, u32[]{:S(2)}) async-start(bf16[4,4,16]{2,1,0:T(4,128)(2,1)} %copy.27), calls=%async_computation.1 | async-start | bytes 8192 | tf_op jit(solution)/shard_map/all_to_all | solution.py:56
  34.0 0.8 %reshape.159 = bf16[16,16,768]{2,1,0:T(8,128)(2,1)} reshape(bf16[16,4,4,768]{3,2,1,0:T(4,128)(2,1)S(1)} %copy.22) | data formatting | bytes 786432 | tf_op jit(solution)/shard_map/reshape | solution.py:52
  34.8 2.8 %all-to-all-done.1 = bf16[4,4,16]{2,1,0:T(4,128)(2,1)S(1)} async-done(((bf16[4,4,16]{2,1,0:T(4,128)(2,1)}), bf16[4,4,16]{2,1,0:T(4,128)(2,1)S(1)}, u32[]{:S(2)}, u32[]{:S(2)}) %all-to-all-start.1) | async-done | bytes 544 | tf_op jit(solution)/shard_map/all_to_all | solution.py:56
  37.6 3.5 %all-to-all-start.3 = ((bf16[16,16,768]{2,1,0:T(8,128)(2,1)}), bf16[16,16,768]{2,1,0:T(8,128)(2,1)S(1)}, u32[]{:S(2)}, u32[]{:S(2)}) async-start(bf16[16,16,768]{2,1,0:T(8,128)(2,1)} %reshape.159), calls=%async_computation.3 | async-start | bytes 786432 | tf_op jit(solution)/shard_map/all_to_all | solution.py:55
  41.2 7.3 %all-to-all-done.3 = bf16[16,16,768]{2,1,0:T(8,128)(2,1)S(1)} async-done(((bf16[16,16,768]{2,1,0:T(8,128)(2,1)}), bf16[16,16,768]{2,1,0:T(8,128)(2,1)S(1)}, u32[]{:S(2)}, u32[]{:S(2)}) %all-to-all-start.3) | async-done | bytes 393248 | tf_op jit(solution)/shard_map/all_to_all | solution.py:55
  48.8 0.6 copy.24
  49.4 3.2 %all-to-all-start.4 = ((f32[4,4,16]{2,0,1:T(4,128)}), f32[4,4,16]{2,0,1:T(4,128)S(1)}, u32[]{:S(2)}, u32[]{:S(2)}) async-start(f32[4,4,16]{2,0,1:T(4,128)} %copy.24), calls=%async_computation.4 | async-start | bytes 16384 | tf_op jit(solution)/shard_map/all_to_all | solution.py:60
  52.7 3.8 %all-to-all-done.4 = f32[4,4,16]{2,0,1:T(4,128)S(1)} async-done(((f32[4,4,16]{2,0,1:T(4,128)}), f32[4,4,16]{2,0,1:T(4,128)S(1)}, u32[]{:S(2)}, u32[]{:S(2)}) %all-to-all-start.4) | async-done | bytes 1056 | tf_op jit(solution)/shard_map/all_to_all | solution.py:60
  56.6 0.7 copy.25
  57.3 3.2 %all-to-all-start.5 = ((f32[16,4,4]{0,2,1:T(4,128)}), f32[16,4,4]{0,2,1:T(4,128)S(1)}, u32[]{:S(2)}, u32[]{:S(2)}) async-start(f32[16,4,4]{0,2,1:T(4,128)} %copy.25), calls=%async_computation.5 | async-start | bytes 16384 | tf_op jit(solution)/shard_map/all_to_all | solution.py:63
  60.5 0.8 %select_reduce_fusion.1 = f32[4,4]{1,0:T(4,128)S(1)} fusion(bf16[4,4,16]{2,1,0:T(4,128)(2,1)} %copy.27, f32[4,4,16]{2,0,1:T(4,128)S(1)} %all-to-all-done.4), kind=kLoop, calls=%fused_computation.18 | loop fusion | flops 752 | bytes 1600 | tf_op jit(solution)/shard_map/reduce_max | solution.py:61
  61.4 6.3 %pmax.7 = f32[16]{0:T(128)} all-reduce(f32[16]{0:T(128)S(1)} %reduce_max.22), channel_id=1, replica_groups=mesh['parts'=2,'wide'=4,'blk'=2,'sub'=2] {'blk','sub'}, use_global_device_ids=true, to_apply=%region_7.8 | all-reduce | flops 16 | bytes 128 | tf_op jit(solution)/shard_map/pmax | solution.py:62
  67.9 2.2 %gather_fusion = f32[192]{0:T(256)} fusion(f32[256]{0:T(256)S(1)} %reshape.161, s32[1024]{0:T(1024)S(1)} %pad_clamp_fusion), kind=kCustom, calls=%fused_computation | custom fusion | bytes 2304 | tf_op jit(solution)/shard_map/gather | solution.py:70
  (28 shorter events, 1.5 us)
Async XLA Ops:
  0.6 1.0 %copy-start.1 = (s32[192]{0:T(256)S(1)}, s32[192]{0:T(256)}, u32[]{:S(2)}) copy-start(s32[192]{0:T(256)} %param.4) | copy-start | bytes 2308
  0.6 1.0 %copy-start.2 = (s32[64]{0:T(128)S(1)}, s32[64]{0:T(128)}, u32[]{:S(2)}) copy-start(s32[64]{0:T(128)} %param.5) | copy-start | bytes 772
  0.6 11.2 %copy-start = (bf16[192,768]{1,0:T(8,128)(2,1)S(1)}, bf16[192,768]{1,0:T(8,128)(2,1)}, u32[]{:S(2)}) copy-start(bf16[192,768]{1,0:T(8,128)(2,1)} %param.3) | copy-start | bytes 884740
  4.4 11.9 %all-to-all-start = ((bf16[16,4,4]{0,2,1:T(4,128)(2,1)}), bf16[16,4,4]{0,2,1:T(4,128)(2,1)S(1)}, u32[]{:S(2)}, u32[]{:S(2)}) async-start(bf16[16,4,4]{0,2,1:T(4,128)(2,1)} %copy.18), calls=%async_computation | async-start | bytes 8192 | tf_op jit(solution)/shard_map/all_to_all | solution.py:50
  16.3 14.3 %all-to-all-start.2 = ((bf16[16,4,4,768]{3,2,0,1:T(4,128)(2,1)}), bf16[16,4,4,768]{3,2,0,1:T(4,128)(2,1)S(1)}, u32[]{:S(2)}, u32[]{:S(2)}) async-start(bf16[16,4,4,768]{3,2,0,1:T(4,128)(2,1)} %copy.21), calls=%async_computation.2 | async-start | bytes 786432 | tf_op jit(solution)/shard_map/all_to_all | solution.py:49
  30.6 7.0 %all-to-all-start.1 = ((bf16[4,4,16]{2,1,0:T(4,128)(2,1)}), bf16[4,4,16]{2,1,0:T(4,128)(2,1)S(1)}, u32[]{:S(2)}, u32[]{:S(2)}) async-start(bf16[4,4,16]{2,1,0:T(4,128)(2,1)} %copy.27), calls=%async_computation.1 | async-start | bytes 8192 | tf_op jit(solution)/shard_map/all_to_all | solution.py:56
  37.6 10.9 %all-to-all-start.3 = ((bf16[16,16,768]{2,1,0:T(8,128)(2,1)}), bf16[16,16,768]{2,1,0:T(8,128)(2,1)S(1)}, u32[]{:S(2)}, u32[]{:S(2)}) async-start(bf16[16,16,768]{2,1,0:T(8,128)(2,1)} %reshape.159), calls=%async_computation.3 | async-start | bytes 786432 | tf_op jit(solution)/shard_map/all_to_all | solution.py:55
  49.4 7.0 %all-to-all-start.4 = ((f32[4,4,16]{2,0,1:T(4,128)}), f32[4,4,16]{2,0,1:T(4,128)S(1)}, u32[]{:S(2)}, u32[]{:S(2)}) async-start(f32[4,4,16]{2,0,1:T(4,128)} %copy.24), calls=%async_computation.4 | async-start | bytes 16384 | tf_op jit(solution)/shard_map/all_to_all | solution.py:60
  57.3 10.4 %all-to-all-start.5 = ((f32[16,4,4]{0,2,1:T(4,128)}), f32[16,4,4]{0,2,1:T(4,128)S(1)}, u32[]{:S(2)}, u32[]{:S(2)}) async-start(f32[16,4,4]{0,2,1:T(4,128)} %copy.25), calls=%async_computation.5 | async-start | bytes 16384 | tf_op jit(solution)/shard_map/all_to_all | solution.py:63
where the time goes:
time: 70.6 us; the launch traced here: 70 us
  waiting for transfers between devices  25.8 us (37%)
  starting transfers between devices  23 us (33%)
  local copies, waits for them, and re-layouts  9.38 us (13%)
  blocking collectives  6.26 us (9%)
  other arithmetic  4.55 us (6%)
  between operations  0.82 us (1%)
    all_to_all x1, waiting for transfers between devices, local(): lax.all_to_all(outgoing, 'wide', split_axis=1, concat_axis=1, tiled=True)  10.1 us
    all_to_all x1, waiting for transfers between devices, local(): lax.all_to_all(arrived, ('blk', 'sub'), split_axis=0, concat_axis=1, tile...  7.27 us
    all_to_all x1, starting transfers between devices, local(): lax.all_to_all(occupied, 'wide', split_axis=1, concat_axis=1, tiled=True)  6.32 us
    pmax x1, blocking collectives, local(): cluster_best = lax.pmax(peak_local, ('blk', 'sub'))  6.26 us
    all_to_all x1, waiting for transfers between devices, local(): lax.all_to_all(single_best, ('blk', 'sub'), split_axis=1, concat_axis=0,...  3.77 us
    all_to_all x1, starting transfers between devices, local(): lax.all_to_all(outgoing, 'wide', split_axis=1, concat_axis=1, tiled=True)  3.46 us
    all_to_all x1, starting transfers between devices, local(): lax.all_to_all(arrived, ('blk', 'sub'), split_axis=0, concat_axis=1, tile...  3.46 us
    all_to_all x1, starting transfers between devices, local(): lax.all_to_all(single_best, ('blk', 'sub'), split_axis=1, concat_axis=0,...  3.25 us
  transfers between devices with their start and end apart: 6, of which 5 were waited for; matrix products, arithmetic and copies ran while one was open for 9% of the time, Pallas kernels for 0%

commit v1 on v0

v1 whole, which is shorter than its diff:
```python
import functools

import jax
import jax.numpy as jnp
from jax import lax
from jax.experimental import pallas as pl
from jax.experimental.pallas import tpu as pltpu
from jax.sharding import PartitionSpec as P

CAP = 4
EPSILON = 1e-06
LOW_MARK = -2.0
UNUSED = 2.0
LANES = 128


def iota(shape, dim):
    return lax.broadcasted_iota(jnp.int32, shape, dim)


def unit_rows(embeddings):
    values = embeddings.astype(jnp.float32)
    squares = jnp.sum(values * values, axis=1, keepdims=True)
    return (values * lax.rsqrt(squares + EPSILON)).astype(jnp.bfloat16)


def kernel(
    sizes, pair, emb_hbm, ids_ref, slot_ref, rowmax_ref, best_ref,
    emb, unit, send, recv, message, answer, load_sem, send_sem, recv_sem, reply_sem, answer_sem,
):
    wide, blk, sub = sizes
    group = blk * sub
    n = wide * group
    rows, width = emb.shape
    clusters = slot_ref.shape[0]
    owned = clusters // n
    me_w, me_b, me_s = lax.axis_index("wide"), lax.axis_index("blk"), lax.axis_index("sub")

    def peer(e, sign):
        dw, db, ds = e // group, (e % group) // sub, e % sub
        return {
            "wide": lax.rem(me_w + sign * dw + wide, wide),
            "blk": lax.rem(me_b + sign * db + blk, blk),
            "sub": lax.rem(me_s + sign * ds + sub, sub),
        }

    def each(lo, hi, body):
        if hi - lo <= 16:
            for e in range(lo, hi):
                body(e)
        else:
            lax.fori_loop(lo, hi, lambda e, c: (body(e), c)[1], 0)

    barrier = pltpu.get_barrier_semaphore()
    each(1, n, lambda e: pl.semaphore_signal(
        barrier, inc=1, device_id=peer(e, 1), device_id_type=pl.DeviceIdType.MESH))

    load = pltpu.make_async_copy(emb_hbm, emb, load_sem)
    load.start()

    ids = ids_ref[...].reshape(1, rows)
    is_cluster = ids == iota((clusters, rows), 0)
    members = is_cluster.astype(jnp.float32)
    earlier = (iota((rows, rows), 0) < iota((rows, rows), 1)).astype(jnp.float32).astype(jnp.bfloat16)
    before = jnp.dot(members.astype(jnp.bfloat16), earlier, preferred_element_type=jnp.float32)
    rank = jnp.sum(members * before, axis=0, keepdims=True).astype(jnp.int32)
    slots = jnp.broadcast_to(slot_ref[...].reshape(1, clusters), (8, clusters)).astype(jnp.float32)
    placed = jnp.dot(slots, members, preferred_element_type=jnp.float32, precision=lax.Precision.HIGHEST)
    placed = (placed[0:1, :] + 0.5).astype(jnp.int32)
    owner, inner = placed // owned, placed % owned

    def offset(coordinate, mine, size):
        gap = coordinate - mine
        return jnp.where(gap < 0, gap + size, gap)

    relative = (
        offset(owner // group, me_w, wide) * group
        + offset(owner % group // sub, me_b, blk) * sub
        + offset(owner % sub, me_s, sub)
    )
    target = relative * pair + inner * CAP + rank

    load.wait()
    unit[...] = unit_rows(emb[...])
    pl.semaphore_wait(barrier, n - 1)

    tile = group * pair
    ones = jnp.ones((rows, LANES), jnp.bfloat16)

    def copy_out(e):
        return pltpu.make_async_remote_copy(
            src_ref=send.at[e], dst_ref=recv.at[e], send_sem=send_sem, recv_sem=recv_sem,
            device_id=peer(e, 1), device_id_type=pl.DeviceIdType.MESH)

    def dispatch(dw):
        pick = (iota((tile, rows), 0) + dw * tile == target).astype(jnp.float32).astype(jnp.bfloat16)
        picked = jnp.dot(pick, unit[...], preferred_element_type=jnp.float32)
        count = jnp.dot(pick, ones, preferred_element_type=jnp.float32)
        head = jnp.where(count > 0.5, picked[:, :LANES], UNUSED).astype(jnp.bfloat16)
        tail = picked[:, LANES:].astype(jnp.bfloat16)
        head = head.reshape(group, pair, LANES)
        tail = tail.reshape(group, pair, width - LANES)
        here = pl.ds(dw * group, group)
        send[here, :, :LANES] = head
        send[here, :, LANES:] = tail
        return head, tail

    def dispatch_far(k):
        ahead = wide - wide // 2
        if isinstance(k, int):
            dw = wide // 2 + k if k < ahead else wide - 1 - k
        else:
            dw = jnp.where(k < ahead, wide // 2 + k, wide - 1 - k)
        dispatch(dw)
        for g in range(group):
            copy_out(dw * group + g).start()

    each(0, wide - 1, dispatch_far)
    head, tail = dispatch(0)
    for g in range(1, group):
        copy_out(g).start()
    recv[0, :, :LANES] = head[0]
    recv[0, :, LANES:] = tail[0]

    others = pl.ds(1, n - 1)
    pltpu.make_async_copy(recv.at[others], recv.at[others], recv_sem).wait()

    total = n * pair
    block = min(total, 256)
    blocks = total // block
    sources = block // pair
    halves = block // LANES

    def load_block(i):
        return recv[pl.ds(i * sources, sources), :, :].reshape(block, width)

    def fold(i, key_block, state):
        queries = load_block(i)
        keys = load_block(key_block)
        scores = lax.dot_general(
            keys, queries, (((1,), (1,)), ((), ())), preferred_element_type=jnp.float32)
        used = keys[:, :LANES].astype(jnp.float32) < 1.5
        key_index = key_block * block + iota((block, LANES), 0)
        out = []
        for h in range(halves):
            best, own = state[h]
            part = scores[:, h * LANES:(h + 1) * LANES]
            index = i * block + h * LANES + iota((block, LANES), 1)
            same = (index % pair) // CAP == (key_index % pair) // CAP
            diagonal = index == key_index
            usable = used & same & jnp.logical_not(diagonal)
            best = jnp.maximum(best, jnp.max(jnp.where(usable, part, LOW_MARK), axis=0, keepdims=True))
            own = jnp.maximum(own, jnp.max(jnp.where(diagonal, part, LOW_MARK), axis=0, keepdims=True))
            out.append((best, own))
        return tuple(out)

    def score(i, peak):
        start = tuple(
            (jnp.full((1, LANES), -1.0, jnp.float32), jnp.full((1, LANES), LOW_MARK, jnp.float32))
            for _ in range(halves))
        if blocks == 1:
            state = fold(0, 0, start)
        else:
            state = lax.fori_loop(0, blocks, lambda j, s: fold(i, j, s), start)
        for h in range(halves):
            best, own = state[h]
            message[i * halves + h, 0:1, :] = best
            peak = jnp.maximum(peak, jnp.where(own < 3.0, best, -1.0))
        return peak

    peak = jnp.full((1, LANES), -1.0, jnp.float32)
    peak = score(0, peak) if blocks == 1 else lax.fori_loop(0, blocks, score, peak)
    depth = max(8, owned)
    lane = iota((depth, LANES), 1)
    level = iota((depth, LANES), 0)
    spread = jnp.max(jnp.where((lane % pair) // CAP == level, peak, -1.0), axis=1, keepdims=True)
    peaks = jnp.max(jnp.where(lane % owned == level, spread, -1.0), axis=0, keepdims=True)
    for c in range(blocks * halves):
        message[c, 1:2, :] = peaks

    per_chunk = LANES // pair

    def reply(e):
        return pltpu.make_async_remote_copy(
            src_ref=message.at[e // per_chunk], dst_ref=answer.at[e], send_sem=reply_sem, recv_sem=answer_sem,
            device_id=peer(e, -1), device_id_type=pl.DeviceIdType.MESH)

    each(1, n, lambda e: reply(e).start())
    answer[0] = message[0]
    pltpu.make_async_copy(answer.at[others], answer.at[others], answer_sem).wait()

    choose = (iota((n, rows), 0) == relative).astype(jnp.float32)
    spreads = lax.dot_general(
        answer[:, 0, :], choose, (((0,), (0,)), ((), ())),
        preferred_element_type=jnp.float32, precision=lax.Precision.HIGHEST)
    hit = iota((LANES, rows), 0) == target % LANES
    result = jnp.sum(jnp.where(hit, spreads, 0.0), axis=0, keepdims=True)
    rowmax_ref[...] = result.reshape(rows)

    span = group * owned
    place = iota((1, LANES), 1) // owned
    near = offset(place // sub, me_b, blk) * sub + offset(place % sub, me_s, sub)
    best = jnp.full((1, LANES), -1.0, jnp.float32)
    for g in range(group):
        best = jnp.where(near == g, answer[g, 1:2, :], best)
    best_ref[...] = best[:, :span].reshape(span)

    pltpu.make_async_copy(send.at[others], send.at[others], send_sem).wait()
    pltpu.make_async_copy(answer.at[others], answer.at[others], reply_sem).wait()


def local(sizes, embeddings, cluster_ids, cluster_slot):
    wide, blk, sub = sizes
    n = wide * blk * sub
    rows, width = embeddings.shape
    clusters = cluster_slot.shape[0]
    pair = -(-(clusters // n * CAP) // 16) * 16
    chunks = n * pair // LANES
    vmem = pl.BlockSpec(memory_space=pltpu.VMEM)
    return pl.pallas_call(
        functools.partial(kernel, sizes, pair),
        out_shape=(
            jax.ShapeDtypeStruct((rows,), jnp.float32),
            jax.ShapeDtypeStruct((clusters // wide,), jnp.float32),
        ),
        in_specs=[pl.BlockSpec(memory_space=pl.ANY), vmem, vmem],
        out_specs=(vmem, vmem),
        scratch_shapes=[
            pltpu.VMEM((rows, width), jnp.bfloat16),
            pltpu.VMEM((rows, width), jnp.bfloat16),
            pltpu.VMEM((n, pair, width), jnp.bfloat16),
            pltpu.VMEM((n, pair, width), jnp.bfloat16),
            pltpu.VMEM((chunks, 2, LANES), jnp.float32),
            pltpu.VMEM((n, 2, LANES), jnp.float32),
            pltpu.SemaphoreType.DMA,
            pltpu.SemaphoreType.DMA,
            pltpu.SemaphoreType.DMA,
            pltpu.SemaphoreType.DMA,
            pltpu.SemaphoreType.DMA,
        ],
        compiler_params=pltpu.CompilerParams(
            collective_id=0, has_side_effects=True,
            vmem_limit_bytes=(16 if n <= 32 else 48) * 1024 * 1024,
        ),
    )(embeddings, cluster_ids, cluster_slot)


def solution(mesh):
    sizes = (mesh.shape["wide"], mesh.shape["blk"], mesh.shape["sub"])
    return jax.shard_map(
        functools.partial(local, sizes),
        mesh=mesh,
        in_specs=(
            P(("parts", "wide", "blk", "sub"), None),
            P(("parts", "wide", "blk", "sub")),
            P("parts"),
        ),
        out_specs=(P(("parts", "wide", "blk", "sub")), P(("parts", "wide"))),
        check_vma=False,
    )
```

time: 70.6 us -> 25.1 us (0.36)
  waiting for transfers between devices: 25.8 us -> 0 us
  starting transfers between devices: 23 us -> 0 us
  Pallas kernels: 0 us -> 20.9 us
  blocking collectives: 6.26 us -> 0 us
  local copies, waits for them, and re-layouts: 9.38 us -> 3.36 us
  other arithmetic: 4.55 us -> 0 us
    all_to_all x6 -> x0, waiting for transfers between devices: 25.8 us -> none  [the longest x1 10.1 us: local(): lax.all_to_all(outgoing, 'wide', split_axis=1, concat_axis=1, tiled=True)]
    all_to_all x6 -> x0, starting transfers between devices: 23 us -> none  [the longest x1 6.32 us: local(): lax.all_to_all(occupied, 'wide', split_axis=1, concat_axis=1, tiled=True)]
    pallas_call x0 -> x1, Pallas kernels: none -> 20.9 us  [local(): pl.pallas_call(functools.partial(kernel, sizes, pair), out_shape=(jax.Sha...]
    pmax x1 -> x0, blocking collectives: 6.26 us -> none  [local(): cluster_best = lax.pmax(peak_local, ('blk', 'sub'))]
    reshape x8 -> x0, local copies, waits for them, and re-layouts: 3.51 us -> none  [the longest x2 0.97 us: local(): outgoing = outgoing.reshape(owned_count, wide_size, CAP, feature_count)]
    unnamed x6 -> x8, local copies, waits for them, and re-layouts: 0.01 us -> 3.36 us
    reduce_sum x3 -> x0, other arithmetic: 2.17 us -> none  [the longest x1 1.1 us: unit_rows(): squares = jnp.sum(values * values, axis=1, keepdims=True)]
    gather x1 -> x0, local copies, waits for them, and re-layouts: 2.17 us -> none  [local(): row_max = returned.reshape(total_slots)[target]]
  transfers between devices with their start and end apart: 6 -> 0, of which waited for: 5 -> 0; matrix products, arithmetic and copies ran while one was open for 9% -> 0% of each run, Pallas kernels for 0% -> 0%
where the time goes in v1:
time: 25.1 us; the launch traced here: 24.9 us
  Pallas kernels  20.9 us (83%)
  local copies, waits for them, and re-layouts  3.36 us (13%)
  between operations  0.65 us (3%)
    pallas_call x1, Pallas kernels, local(): pl.pallas_call(functools.partial(kernel, sizes, pair), out_shape=(jax.Sha...  20.9 us
    unnamed x8, local copies, waits for them, and re-layouts  3.36 us

profile of v1, /device:TPU:0, one launch (start us, length us, event | category | flops | bytes accessed | tf_op | source)
XLA Modules:
  0.0 24.9 jit_solution(9727730270659352297)
XLA Ops:
  0.6 0.0 copy-start
  0.6 1.0 %copy-done = bf16[192,768]{1,0:T(8,128)(2,1)S(1)} copy-done((bf16[192,768]{1,0:T(8,128)(2,1)S(1)}, bf16[192,768]{1,0:T(8,128)(2,1)}, u32[]{:S(2)}) %copy-start) | copy-done | bytes 294936
  1.6 0.0 copy-start.1
  1.6 0.7 %copy-done.1 = s32[192]{0:T(256)S(1)} copy-done((s32[192]{0:T(256)S(1)}, s32[192]{0:T(256)}, u32[]{:S(2)}) %copy-start.1) | copy-done | bytes 792
  2.3 0.0 copy-start.2
  2.3 0.7 %copy-done.2 = s32[64]{0:T(128)S(1)} copy-done((s32[64]{0:T(128)S(1)}, s32[64]{0:T(128)}, u32[]{:S(2)}) %copy-start.2) | copy-done | bytes 280
  2.9 20.9 %shard_map.50 = (f32[192]{0:T(256)S(1)}, f32[16]{0:T(128)S(1)}) custom-call(bf16[192,768]{1,0:T(8,128)(2,1)S(1)} %copy-done, s32[192]{0:T(256)S(1)} %copy-done.1, s32[64]{0:T(128)S(1)} %copy-done.2), custom_call_target="tpu_custom_call" | custom-call | tf_op jit(solution)/shard_map/pallas_call | solution.py:220
  23.8 0.6 %copy.7 = f32[192]{0:T(256)} copy(f32[192]{0:T(256)S(1)} %get-tuple-element.4) | data formatting | bytes 1536
  24.4 0.5 %copy.8 = f32[16]{0:T(128)} copy(f32[16]{0:T(128)S(1)} %get-tuple-element.5) | data formatting | bytes 128
Async XLA Ops:
  0.6 1.0 %copy-start = (bf16[192,768]{1,0:T(8,128)(2,1)S(1)}, bf16[192,768]{1,0:T(8,128)(2,1)}, u32[]{:S(2)}) copy-start(bf16[192,768]{1,0:T(8,128)(2,1)} %emb_hbm.1) | copy-start | bytes 884740
  1.6 0.7 %copy-start.1 = (s32[192]{0:T(256)S(1)}, s32[192]{0:T(256)}, u32[]{:S(2)}) copy-start(s32[192]{0:T(256)} %ids_ref.1) | copy-start | bytes 2308
  2.3 0.7 %copy-start.2 = (s32[64]{0:T(128)S(1)}, s32[64]{0:T(128)}, u32[]{:S(2)}) copy-start(s32[64]{0:T(128)} %slot_ref.1) | copy-start | bytes 772

commit v2 on v1

--- a/solution.py
+++ b/solution.py
@@ -25,8 +25,8 @@
 
 
 def kernel(
-    sizes, pair, emb_hbm, ids_ref, slot_ref, rowmax_ref, best_ref,
-    emb, unit, send, recv, message, answer, load_sem, send_sem, recv_sem, reply_sem, answer_sem,
+    sizes, pair, emb_hbm, ids_hbm, slot_hbm, rowmax_ref, best_ref,
+    ids_ref, slot_ref, emb, unit, send, recv, message, answer, ids_sem, slot_sem, load_sem, send_sem, recv_sem, reply_sem, answer_sem,
 ):
     wide, blk, sub = sizes
     group = blk * sub
@@ -51,13 +51,19 @@
         else:
             lax.fori_loop(lo, hi, lambda e, c: (body(e), c)[1], 0)
 
+    load_ids = pltpu.make_async_copy(ids_hbm, ids_ref, ids_sem)
+    load_slots = pltpu.make_async_copy(slot_hbm, slot_ref, slot_sem)
+    load = pltpu.make_async_copy(emb_hbm, emb, load_sem)
+    load_ids.start()
+    load_slots.start()
+    load.start()
     barrier = pltpu.get_barrier_semaphore()
     each(1, n, lambda e: pl.semaphore_signal(
         barrier, inc=1, device_id=peer(e, 1), device_id_type=pl.DeviceIdType.MESH))
 
-    load = pltpu.make_async_copy(emb_hbm, emb, load_sem)
-    load.start()
-
+
+    load_ids.wait()
+    load_slots.wait()
     ids = ids_ref[...].reshape(1, rows)
     is_cluster = ids == iota((clusters, rows), 0)
     members = is_cluster.astype(jnp.float32)
@@ -220,12 +226,14 @@
     return pl.pallas_call(
         functools.partial(kernel, sizes, pair),
         out_shape=(
-            jax.ShapeDtypeStruct((rows,), jnp.float32),
-            jax.ShapeDtypeStruct((clusters // wide,), jnp.float32),
+            pltpu.VMEM((rows,), jnp.float32),
+            pltpu.VMEM((clusters // wide,), jnp.float32),
         ),
-        in_specs=[pl.BlockSpec(memory_space=pl.ANY), vmem, vmem],
+        in_specs=[pl.BlockSpec(memory_space=pltpu.HBM)] * 3,
         out_specs=(vmem, vmem),
         scratch_shapes=[
+            pltpu.VMEM((rows,), jnp.int32),
+            pltpu.VMEM((clusters,), jnp.int32),
             pltpu.VMEM((rows, width), jnp.bfloat16),
             pltpu.VMEM((rows, width), jnp.bfloat16),
             pltpu.VMEM((n, pair, width), jnp.bfloat16),
@@ -237,10 +245,12 @@
             pltpu.SemaphoreType.DMA,
             pltpu.SemaphoreType.DMA,
             pltpu.SemaphoreType.DMA,
+            pltpu.SemaphoreType.DMA,
+            pltpu.SemaphoreType.DMA,
         ],
         compiler_params=pltpu.CompilerParams(
             collective_id=0, has_side_effects=True,
-            vmem_limit_bytes=(16 if n <= 32 else 48) * 1024 * 1024,
+            vmem_limit_bytes=56 * 1024 * 1024,
         ),
     )(embeddings, cluster_ids, cluster_slot)
 

time: 25.1 us -> 22.9 us (0.912)
  local copies, waits for them, and re-layouts: 3.36 us -> 1.08 us
    unnamed x8 -> x2, local copies, waits for them, and re-layouts: 3.36 us -> 1.08 us
where the time goes in v2:
time: 22.9 us; the launch traced here: 22.7 us
  Pallas kernels  21 us (92%)
  local copies, waits for them, and re-layouts  1.08 us (5%)
  between operations  0.64 us (3%)
    pallas_call x1, Pallas kernels, local(): pl.pallas_call(functools.partial(kernel, sizes, pair), out_shape=(pltpu.V...  21 us
    unnamed x2, local copies, waits for them, and re-layouts  1.08 us

profile of v2, /device:TPU:0, one launch (start us, length us, event | category | flops | bytes accessed | tf_op | source)
XLA Modules:
  0.0 22.7 jit_solution(496106665307782684)
XLA Ops:
  0.6 21.0 %shard_map.50 = (f32[192]{0:T(256)S(1)}, f32[16]{0:T(128)S(1)}) custom-call(bf16[192,768]{1,0:T(8,128)(2,1)} %emb_hbm.1, s32[192]{0:T(256)} %ids_hbm.1, s32[64]{0:T(128)} %slot_hbm.1), custom_call_target="tpu_custom_call" | custom-call | tf_op jit(solution)/shard_map/pallas_call | solution.py:226
  21.7 0.6 %copy.7 = f32[192]{0:T(256)} copy(f32[192]{0:T(256)S(1)} %get-tuple-element.2) | data formatting | bytes 1536
  22.2 0.5 %copy.8 = f32[16]{0:T(128)} copy(f32[16]{0:T(128)S(1)} %get-tuple-element.3) | data formatting | bytes 128

commit v3 on v2

--- a/solution.py
+++ b/solution.py
@@ -98,6 +98,8 @@
             src_ref=send.at[e], dst_ref=recv.at[e], send_sem=send_sem, recv_sem=recv_sem,
             device_id=peer(e, 1), device_id_type=pl.DeviceIdType.MESH)
 
+    across = [*range(group // 2, group), *range(group // 2)]
+
     def dispatch(dw):
         pick = (iota((tile, rows), 0) + dw * tile == target).astype(jnp.float32).astype(jnp.bfloat16)
         picked = jnp.dot(pick, unit[...], preferred_element_type=jnp.float32)
@@ -118,7 +120,7 @@
         else:
             dw = jnp.where(k < ahead, wide // 2 + k, wide - 1 - k)
         dispatch(dw)
-        for g in range(group):
+        for g in across:
             copy_out(dw * group + g).start()
 
     each(0, wide - 1, dispatch_far)
@@ -215,6 +217,30 @@
     pltpu.make_async_copy(answer.at[others], answer.at[others], reply_sem).wait()
 
 
+def forward(row_in, best_in, row_out, best_out, row_sem, best_sem):
+    first = pltpu.make_async_copy(row_in, row_out, row_sem)
+    second = pltpu.make_async_copy(best_in, best_out, best_sem)
+    first.start()
+    second.start()
+    first.wait()
+    second.wait()
+
+
+def finish(row_max, cluster_best):
+    anywhere = pl.BlockSpec(memory_space=pl.ANY)
+    return pl.pallas_call(
+        forward,
+        out_shape=(
+            jax.ShapeDtypeStruct(row_max.shape, jnp.float32),
+            jax.ShapeDtypeStruct(cluster_best.shape, jnp.float32),
+        ),
+        in_specs=[pl.BlockSpec(memory_space=pltpu.VMEM)] * 2,
+        out_specs=(pl.BlockSpec(memory_space=pltpu.HBM),) * 2,
+        scratch_shapes=[pltpu.SemaphoreType.DMA, pltpu.SemaphoreType.DMA],
+        compiler_params=pltpu.CompilerParams(vmem_limit_bytes=1024 * 1024),
+    )(row_max, cluster_best)
+
+
 def local(sizes, embeddings, cluster_ids, cluster_slot):
     wide, blk, sub = sizes
     n = wide * blk * sub
@@ -223,7 +249,7 @@
     pair = -(-(clusters // n * CAP) // 16) * 16
     chunks = n * pair // LANES
     vmem = pl.BlockSpec(memory_space=pltpu.VMEM)
-    return pl.pallas_call(
+    return finish(*pl.pallas_call(
         functools.partial(kernel, sizes, pair),
         out_shape=(
             pltpu.VMEM((rows,), jnp.float32),
@@ -252,7 +278,7 @@
             collective_id=0, has_side_effects=True,
             vmem_limit_bytes=56 * 1024 * 1024,
         ),
-    )(embeddings, cluster_ids, cluster_slot)
+    )(embeddings, cluster_ids, cluster_slot))
 
 
 def solution(mesh):

time: 22.9 us -> 21.6 us (0.943)
  local copies, waits for them, and re-layouts: 1.08 us -> 0 us
    unnamed x2 -> x0, local copies, waits for them, and re-layouts: 1.08 us -> none
    pallas_call x1, Pallas kernels: 21 us -> 20.2 us  [local(): pl.pallas_call(functools.partial(kernel, sizes, pair), out_shape=(pltpu.V...]
    pallas_call x0 -> x1, Pallas kernels: none -> 0.58 us  [finish(): pl.pallas_call(forward, out_shape=(jax.ShapeDtypeStruct(row_max.shape, jn...]
where the time goes in v3:
time: 21.6 us; the launch traced here: 21.4 us
  Pallas kernels  20.8 us (96%)
  between operations  0.64 us (3%)
    pallas_call x1, Pallas kernels, local(): pl.pallas_call(functools.partial(kernel, sizes, pair), out_shape=(pltpu.V...  20.2 us
    pallas_call x1, Pallas kernels, finish(): pl.pallas_call(forward, out_shape=(jax.ShapeDtypeStruct(row_max.shape, jn...  0.58 us

profile of v3, /device:TPU:0, one launch (start us, length us, event | category | flops | bytes accessed | tf_op | source)
XLA Modules:
  0.0 21.4 jit_solution(10112156782832297115)
XLA Ops:
  0.6 20.2 %shard_map.50 = (f32[192]{0:T(256)S(1)}, f32[16]{0:T(128)S(1)}) custom-call(bf16[192,768]{1,0:T(8,128)(2,1)} %emb_hbm.1, s32[192]{0:T(256)} %ids_hbm.1, s32[64]{0:T(128)} %slot_hbm.1), custom_call_target="tpu_custom_call" | custom-call | tf_op jit(solution)/shard_map/pallas_call | solution.py:252
  20.8 0.6 %shard_map.51 = (f32[192]{0:T(256)}, f32[16]{0:T(128)}) custom-call(f32[192]{0:T(256)S(1)} %get-tuple-element.4.row_in, f32[16]{0:T(128)S(1)} %get-tuple-element.5.best_in), custom_call_target="tpu_custom_call" | custom-call | tf_op jit(solution)/shard_map/pallas_call | solution.py:231

commit v4 on v3

--- a/solution.py
+++ b/solution.py
@@ -26,7 +26,7 @@
 
 def kernel(
     sizes, pair, emb_hbm, ids_hbm, slot_hbm, rowmax_ref, best_ref,
-    ids_ref, slot_ref, emb, unit, send, recv, message, answer, ids_sem, slot_sem, load_sem, send_sem, recv_sem, reply_sem, answer_sem,
+    ids_ref, slot_ref, emb, unit, send, recv, message, answer, peak_out, peak_in, tell_sem, peak_sem, ids_sem, slot_sem, load_sem, send_sem, recv_sem, reply_sem, answer_sem,
 ):
     wide, blk, sub = sizes
     group = blk * sub
@@ -70,9 +70,11 @@
     earlier = (iota((rows, rows), 0) < iota((rows, rows), 1)).astype(jnp.float32).astype(jnp.bfloat16)
     before = jnp.dot(members.astype(jnp.bfloat16), earlier, preferred_element_type=jnp.float32)
     rank = jnp.sum(members * before, axis=0, keepdims=True).astype(jnp.int32)
-    slots = jnp.broadcast_to(slot_ref[...].reshape(1, clusters), (8, clusters)).astype(jnp.float32)
-    placed = jnp.dot(slots, members, preferred_element_type=jnp.float32, precision=lax.Precision.HIGHEST)
-    placed = (placed[0:1, :] + 0.5).astype(jnp.int32)
+    slots = jnp.broadcast_to(slot_ref[...].reshape(1, clusters), (8, clusters))
+    low = slots % 128
+    slots = jnp.where(iota((8, clusters), 0) == 0, low, slots - low).astype(jnp.float32).astype(jnp.bfloat16)
+    placed = jnp.dot(slots, members.astype(jnp.bfloat16), preferred_element_type=jnp.float32)
+    placed = (placed[0:1, :] + placed[1:2, :] + 0.5).astype(jnp.int32)
     owner, inner = placed // owned, placed % owned
 
     def offset(coordinate, mine, size):
@@ -172,49 +174,66 @@
             state = lax.fori_loop(0, blocks, lambda j, s: fold(i, j, s), start)
         for h in range(halves):
             best, own = state[h]
-            message[i * halves + h, 0:1, :] = best
+            message[i * halves + h] = best
             peak = jnp.maximum(peak, jnp.where(own < 3.0, best, -1.0))
         return peak
 
     peak = jnp.full((1, LANES), -1.0, jnp.float32)
     peak = score(0, peak) if blocks == 1 else lax.fori_loop(0, blocks, score, peak)
+    per_chunk = LANES // pair
+
+    def reply(e):
+        return pltpu.make_async_remote_copy(
+            src_ref=message.at[e // per_chunk], dst_ref=answer.at[e], send_sem=reply_sem, recv_sem=answer_sem,
+            device_id=peer(e, -1), device_id_type=pl.DeviceIdType.MESH)
+
+    each(1, n, lambda e: reply(n - e).start())
+    answer[0] = message[0]
     depth = max(8, owned)
     lane = iota((depth, LANES), 1)
     level = iota((depth, LANES), 0)
     spread = jnp.max(jnp.where((lane % pair) // CAP == level, peak, -1.0), axis=1, keepdims=True)
     peaks = jnp.max(jnp.where(lane % owned == level, spread, -1.0), axis=0, keepdims=True)
-    for c in range(blocks * halves):
-        message[c, 1:2, :] = peaks
-
-    per_chunk = LANES // pair
-
-    def reply(e):
+    peak_out[...] = peaks
+
+    def tell(g):
         return pltpu.make_async_remote_copy(
-            src_ref=message.at[e // per_chunk], dst_ref=answer.at[e], send_sem=reply_sem, recv_sem=answer_sem,
-            device_id=peer(e, -1), device_id_type=pl.DeviceIdType.MESH)
-
-    each(1, n, lambda e: reply(e).start())
-    answer[0] = message[0]
+            src_ref=peak_out, dst_ref=peak_in.at[g], send_sem=tell_sem, recv_sem=peak_sem,
+            device_id=peer(g, -1), device_id_type=pl.DeviceIdType.MESH)
+
+    for g in range(1, group):
+        tell(g).start()
+    peak_in[0] = peaks
+
+    choose = (iota((n, rows), 0) == relative).astype(jnp.float32).astype(jnp.bfloat16)
+    choose = jnp.concatenate([choose, choose, choose], axis=0)
+    hit = iota((LANES, rows), 0) == target % LANES
     pltpu.make_async_copy(answer.at[others], answer.at[others], answer_sem).wait()
 
-    choose = (iota((n, rows), 0) == relative).astype(jnp.float32)
+    values = answer[:, 0, :]
+    high = values.astype(jnp.bfloat16)
+    rest = values - high.astype(jnp.float32)
+    middle = rest.astype(jnp.bfloat16)
+    lowest = (rest - middle.astype(jnp.float32)).astype(jnp.bfloat16)
     spreads = lax.dot_general(
-        answer[:, 0, :], choose, (((0,), (0,)), ((), ())),
-        preferred_element_type=jnp.float32, precision=lax.Precision.HIGHEST)
-    hit = iota((LANES, rows), 0) == target % LANES
+        jnp.concatenate([high, middle, lowest], axis=0), choose, (((0,), (0,)), ((), ())),
+        preferred_element_type=jnp.float32)
     result = jnp.sum(jnp.where(hit, spreads, 0.0), axis=0, keepdims=True)
     rowmax_ref[...] = result.reshape(rows)
 
     span = group * owned
     place = iota((1, LANES), 1) // owned
     near = offset(place // sub, me_b, blk) * sub + offset(place % sub, me_s, sub)
+    near_others = pl.ds(1, group - 1)
+    pltpu.make_async_copy(peak_in.at[near_others], peak_in.at[near_others], peak_sem).wait()
     best = jnp.full((1, LANES), -1.0, jnp.float32)
     for g in range(group):
-        best = jnp.where(near == g, answer[g, 1:2, :], best)
+        best = jnp.where(near == g, peak_in[g], best)
     best_ref[...] = best[:, :span].reshape(span)
 
     pltpu.make_async_copy(send.at[others], send.at[others], send_sem).wait()
     pltpu.make_async_copy(answer.at[others], answer.at[others], reply_sem).wait()
+    pltpu.make_async_copy(peak_in.at[near_others], peak_in.at[near_others], tell_sem).wait()
 
 
 def forward(row_in, best_in, row_out, best_out, row_sem, best_sem):
@@ -264,8 +283,12 @@
             pltpu.VMEM((rows, width), jnp.bfloat16),
             pltpu.VMEM((n, pair, width), jnp.bfloat16),
             pltpu.VMEM((n, pair, width), jnp.bfloat16),
-            pltpu.VMEM((chunks, 2, LANES), jnp.float32),
-            pltpu.VMEM((n, 2, LANES), jnp.float32),
+            pltpu.VMEM((chunks, 1, LANES), jnp.float32),
+            pltpu.VMEM((n, 1, LANES), jnp.float32),
+            pltpu.VMEM((1, LANES), jnp.float32),
+            pltpu.VMEM((blk * sub, 1, LANES), jnp.float32),
+            pltpu.SemaphoreType.DMA,
+            pltpu.SemaphoreType.DMA,
             pltpu.SemaphoreType.DMA,
             pltpu.SemaphoreType.DMA,
             pltpu.SemaphoreType.DMA,

time: 21.6 us -> 21.2 us (0.981)
  Pallas kernels: 20.8 us -> 20.4 us
    pallas_call x1, Pallas kernels: 20.2 us -> 19.8 us  [local(): pl.pallas_call(functools.partial(kernel, sizes, pair), out_shape=(pltpu.V...]
where the time goes in v4:
time: 21.2 us; the launch traced here: 21 us
  Pallas kernels  20.4 us (96%)
  between operations  0.64 us (3%)
    pallas_call x1, Pallas kernels, local(): pl.pallas_call(functools.partial(kernel, sizes, pair), out_shape=(pltpu.V...  19.8 us
    pallas_call x1, Pallas kernels, finish(): pl.pallas_call(forward, out_shape=(jax.ShapeDtypeStruct(row_max.shape, jn...  0.58 us

profile of v4, /device:TPU:0, one launch (start us, length us, event | category | flops | bytes accessed | tf_op | source)
XLA Modules:
  0.0 21.0 jit_solution(1451423427269233864)
XLA Ops:
  0.6 19.8 %shard_map.50 = (f32[192]{0:T(256)S(1)}, f32[16]{0:T(128)S(1)}) custom-call(bf16[192,768]{1,0:T(8,128)(2,1)} %emb_hbm.1, s32[192]{0:T(256)} %ids_hbm.1, s32[64]{0:T(128)} %slot_hbm.1), custom_call_target="tpu_custom_call" | custom-call | tf_op jit(solution)/shard_map/pallas_call | solution.py:271
  20.5 0.6 %shard_map.51 = (f32[192]{0:T(256)}, f32[16]{0:T(128)}) custom-call(f32[192]{0:T(256)S(1)} %get-tuple-element.4.row_in, f32[16]{0:T(128)S(1)} %get-tuple-element.5.best_in), custom_call_target="tpu_custom_call" | custom-call | tf_op jit(solution)/shard_map/pallas_call | solution.py:250

commit v5 on v4

--- a/solution.py
+++ b/solution.py
@@ -90,7 +90,6 @@
 
     load.wait()
     unit[...] = unit_rows(emb[...])
-    pl.semaphore_wait(barrier, n - 1)
 
     tile = group * pair
     ones = jnp.ones((rows, LANES), jnp.bfloat16)
@@ -125,7 +124,11 @@
         for g in across:
             copy_out(dw * group + g).start()
 
-    each(0, wide - 1, dispatch_far)
+    dispatch(wide // 2)
+    pl.semaphore_wait(barrier, n - 1)
+    for g in across:
+        copy_out(wide // 2 * group + g).start()
+    each(1, wide - 1, dispatch_far)
     head, tail = dispatch(0)
     for g in range(1, group):
         copy_out(g).start()

time: 21.2 us -> 21 us (level)
  no operation moved by 1% of the time
where the time goes in v5:
time: 21 us; the launch traced here: 20.8 us
  Pallas kernels  20.2 us (96%)
  between operations  0.64 us (3%)
    pallas_call x1, Pallas kernels, local(): pl.pallas_call(functools.partial(kernel, sizes, pair), out_shape=(pltpu.V...  19.6 us
    pallas_call x1, Pallas kernels, finish(): pl.pallas_call(forward, out_shape=(jax.ShapeDtypeStruct(row_max.shape, jn...  0.58 us

profile of v5, /device:TPU:0, one launch (start us, length us, event | category | flops | bytes accessed | tf_op | source)
XLA Modules:
  0.0 20.8 jit_solution(12286422393232918703)
XLA Ops:
  0.6 19.6 %shard_map.50 = (f32[192]{0:T(256)S(1)}, f32[16]{0:T(128)S(1)}) custom-call(bf16[192,768]{1,0:T(8,128)(2,1)} %emb_hbm.1, s32[192]{0:T(256)} %ids_hbm.1, s32[64]{0:T(128)} %slot_hbm.1), custom_call_target="tpu_custom_call" | custom-call | tf_op jit(solution)/shard_map/pallas_call | solution.py:274
  20.3 0.6 %shard_map.51 = (f32[192]{0:T(256)}, f32[16]{0:T(128)}) custom-call(f32[192]{0:T(256)S(1)} %get-tuple-element.4.row_in, f32[16]{0:T(128)S(1)} %get-tuple-element.5.best_in), custom_call_target="tpu_custom_call" | custom-call | tf_op jit(solution)/shard_map/pallas_call | solution.py:253
